TPU v7x, 256 devices: a whole 4x4x8 slice. The times are simulated.
256 devices in a mesh: stn: 32 (over x, z_lo, core), band: 8 (over z_hi, y).
Axes of the slice: x: 4, y: 4, z: 8 (z_hi: 2, z_lo: 4; z = z_hi * 4 + z_lo), core: 2. Of those that a mesh axis runs over, the one named last changes fastest.
Arguments:
- voltages: bfloat16 [8, 2, 512, 36608], P('band', None, 'stn'), may hold values from -6 to 6
- taps: float32 [16, 256], replicated, may hold values from -1.5 to 1.5
- flags: int32 [512], P('stn'), may hold values 0 or 1
- steer: bfloat16 [256, 2, 256, 256], P('band', None, 'stn'), may hold values from -0.25 to 0.25
- beam_dirs: int32 [128], replicated, may hold values from 0 to 255
Outputs:
- visibilities: bfloat16 [8, 256, 2, 512, 512], P('band', 'stn')
- beams: bfloat16 [8, 256, 2, 2, 128, 128], P('band', 'stn')
Inputs may be any that keep to these rules, and one draw needn't show every extreme that they name: `beam_dirs`: each beam names a row of steer.
All inputs are finite; a program needn't handle non-finite values. No bound on the sum of `flags` on one device may be relied on, other than what follows from the above.
Results may differ from a plain program's by a relative error of at most 0.0071.
Values may be sent and summed in bfloat16 or wider, within the bound.
A program may use at most 64 MiB of HBM per device.

v0:
```python
import math

import jax
import jax.numpy as jnp
from jax import lax
from jax.sharding import PartitionSpec as P


def dft_matrix_of(chan_len):
    indices = jnp.arange(chan_len, dtype=jnp.int32)
    phase_step = indices[:, None] * indices[None, :] % chan_len
    angle = phase_step.astype(jnp.float32) * (2.0 * math.pi / chan_len)
    normaliser = 1.0 / math.sqrt(chan_len)
    cosine_part = jnp.cos(angle) * normaliser
    sine_part = jnp.sin(angle) * normaliser
    upper_rows = jnp.stack([cosine_part, -sine_part], axis=1)
    lower_rows = jnp.stack([sine_part, cosine_part], axis=1)
    return jnp.stack([upper_rows, lower_rows], axis=0).astype(jnp.bfloat16)


def correlate(spectrum, weights, frames_count):
    count_in = spectrum.shape[1]
    stacked = spectrum.reshape(2 * count_in, frames_count)
    products = lax.dot_general(
        stacked, stacked, (((1,), (1,)), ((), ())), preferred_element_type=jnp.float32
    )
    real_part = products[:count_in, :count_in] + products[count_in:, count_in:]
    imag_part = products[count_in:, :count_in] - products[:count_in, count_in:]
    visible = (jnp.stack([real_part, imag_part]) / frames_count).astype(jnp.bfloat16)
    weight_real = weights[:, 0, :]
    weight_imag = weights[:, 1, :]
    weight_block = jnp.concatenate(
        [
            jnp.concatenate([weight_real, -weight_imag], axis=1),
            jnp.concatenate([weight_imag, weight_real], axis=1),
        ],
        axis=0,
    )
    by_pol = spectrum.reshape(2, count_in // 2, 2, frames_count)
    formed = []
    for polarisation in range(2):
        pol_rows = by_pol[:, :, polarisation, :].reshape(count_in, frames_count)
        beam_pol = jnp.dot(weight_block, pol_rows, preferred_element_type=jnp.float32)
        formed.append(beam_pol.reshape(2, weights.shape[0], frames_count))
    return (visible, jnp.stack(formed, axis=1).astype(jnp.bfloat16))


def body(voltages, taps, flags, steer, beam_dirs):
    samples = voltages[0]
    tap_count, chan_len = taps.shape
    local_inputs = samples.shape[1]
    frames = samples.reshape(2, local_inputs, -1, chan_len)
    frames_count = frames.shape[2] - tap_count + 1
    filtered = jnp.zeros((2, local_inputs, frames_count, chan_len), jnp.float32)
    for tap_step in range(tap_count):
        filtered = filtered + taps[tap_step] * frames[
            :, :, tap_step : tap_step + frames_count, :
        ].astype(jnp.float32)
    filtered = filtered.astype(jnp.bfloat16)
    spectra = jnp.einsum(
        "sifk,skoc->oicf", filtered, dft_matrix_of(chan_len), preferred_element_type=jnp.float32
    )
    spectra = spectra.astype(jnp.bfloat16) * flags.astype(jnp.bfloat16)[None, :, None, None]
    turned = lax.all_to_all(spectra, "stn", split_axis=2, concat_axis=1, tiled=True)
    chan_count = turned.shape[2]
    gathered = lax.all_gather(steer, "band", axis=0, tiled=True)
    picked = jnp.take(gathered, beam_dirs, axis=0)
    picked = jnp.transpose(picked, (2, 0, 1, 3))

    def one_channel(channel):
        spectrum = lax.dynamic_index_in_dim(turned, channel, 2, keepdims=False)
        weights = lax.dynamic_index_in_dim(picked, channel, 0, keepdims=False)
        return correlate(spectrum, weights, frames_count)

    visibilities, beams = lax.map(one_channel, jnp.arange(chan_count, dtype=jnp.int32))
    return (visibilities[None], beams[None])


def solution(mesh):
    return jax.shard_map(
        body,
        mesh=mesh,
        in_specs=(P("band", None, "stn", None), P(), P("stn"), P("band", None, "stn", None), P()),
        out_specs=(P("band", "stn", None, None, None), P("band", "stn", None, None, None, None)),
        check_vma=False,
    )
```

profile of v0, /device:TPU:35, one launch (start us, length us, event | category | flops | bytes accessed | tf_op | source)
XLA Modules:
  0.0 188.0 jit_solution(5803599424780491543)
XLA Ops:
  7.2 1.0 fusion.19
  8.2 1.1 negate_convert_fusion
  9.3 0.7 convert_element_type.120
  9.9 1.0 fusion.22
  11.0 3.1 %reshape_squeeze.3 = bf16[2,16,143,256]{3,2,1,0:T(8,128)(2,1)S(1)} reshape(bf16[1,2,16,36608]{3,2,1,0:T(8,128)(2,1)} %param.7) | data formatting | bytes 4685824 | tf_op jit(solution)/shard_map/reshape;squeeze | solution.py:52
  14.2 9.8 %multiply_bitcast_fusion = bf16[2,16,256,128]{3,2,1,0:T(8,128)(2,1)S(1)} fusion(bf16[16]{0:T(256)(128)(2,1)S(1)} %convert_element_type.120, bf16[1,256,2,256]{1,3,0,2:T(8,128)(2,1)S(1)} %get-tuple-element.74, bf16[1,256,2,256]{1,3,0,2:T(8,128)(2,1)S(1)} %get-tuple-element.73, bf16[2,16,143,256]{3,2,1,0:T(8,128)(2,1)S(1)} %reshape_squeeze.3, ...), kind=kOutput, calls=%fused_computation.24 | convolution fusion | flops 1127219200 | bytes 36192768 | tf_op jit(solution)/shard_map/sifk,skoc->oicf/dot_general | solution.py:60
  24.0 2.7 %copy.38 = bf16[2,16,256,128]{3,1,0,2:T(8,128)(2,1)} copy(bf16[2,16,256,128]{3,2,1,0:T(8,128)(2,1)S(1)} %multiply_bitcast_fusion) | data formatting | bytes 4194304 | tf_op jit(solution)/shard_map/mul | solution.py:63
  26.6 8.9 %all-to-all-start = ((bf16[2,16,256,128]{3,1,0,2:T(8,128)(2,1)}), bf16[2,16,256,128]{3,1,0,2:T(8,128)(2,1)S(1)}, u32[]{:S(2)}, u32[]{:S(2)}) async-start(bf16[2,16,256,128]{3,1,0,2:T(8,128)(2,1)} %copy.38), calls=%async_computation | async-start | bytes 4194304 | tf_op jit(solution)/shard_map/all_to_all | solution.py:64
  36.4 82.0 %all-gather.2.cloned.1.call-done = bf16[256,2,8,256]{3,2,1,0:T(8,128)(2,1)} async-done(((bf16[32,2,8,256]{3,2,1,0:T(8,128)(2,1)}), bf16[256,2,8,256]{3,2,1,0:T(8,128)(2,1)}) %all-gather.2.cloned.1.call-update) | async-done | bytes 2097168 | tf_op jit(solution)/shard_map/all_gather | solution.py:66
  118.4 2.2 %gather_fusion = bf16[128,2,8,256]{3,2,1,0:T(8,128)(2,1)S(1)} fusion(bf16[256,2,8,256]{3,2,1,0:T(8,128)(2,1)} %all-gather.2.cloned.1.call-done, s32[1024]{0:T(1024)S(1)} %pad_clamp_fusion), kind=kCustom, calls=%fused_computation | custom fusion | bytes 2097664 | tf_op jit(solution)/shard_map/jit(_take)/gather | solution.py:67
  121.2 1.9 copy.39
  123.1 58.0 %while.12 = (s32[]{:T(128)}, bf16[8,2,512,512]{3,2,1,0:T(8,128)(2,1)}, bf16[8,2,2,128,128]{4,3,2,1,0:T(8,128)(2,1)}, s32[8]{0:T(128)S(1)}, bf16[2,512,8,128]{3,1...) while((s32[]{:T(128)}, ...), condition=%wide.region_1.2_spmd, body=%wide.region_0.1_spmd.sunk | while | flops 338853888 | bytes 17760420 | solution.py:75
  123.1 0.6 dynamic_slice.19
  125.4 1.0 constant_dynamic-slice_fusion.2
  127.2 0.7 copy_dynamic-update-slice_fusion.2
  127.9 0.7 fusion.49
  129.1 1.3 fusion.51
  130.4 0.6 dynamic_slice.19
  132.7 1.0 constant_dynamic-slice_fusion.2
  134.5 0.7 copy_dynamic-update-slice_fusion.2
  135.2 0.7 fusion.49
  136.4 1.3 fusion.51
  139.9 1.0 constant_dynamic-slice_fusion.2
  141.8 0.7 copy_dynamic-update-slice_fusion.2
  142.4 0.7 fusion.49
  143.6 1.3 fusion.51
  147.2 1.0 constant_dynamic-slice_fusion.2
  149.0 0.7 copy_dynamic-update-slice_fusion.2
  149.7 0.7 fusion.49
  150.9 1.3 fusion.51
  154.4 1.0 constant_dynamic-slice_fusion.2
  156.3 0.7 copy_dynamic-update-slice_fusion.2
  156.9 0.7 fusion.49
  158.1 1.3 fusion.51
  159.4 0.6 dynamic_slice.19
  161.7 1.0 constant_dynamic-slice_fusion.2
  163.5 0.7 copy_dynamic-update-slice_fusion.2
  164.2 0.7 fusion.49
  165.4 1.3 fusion.51
  166.6 0.6 dynamic_slice.19
  168.9 1.0 constant_dynamic-slice_fusion.2
  170.8 0.7 copy_dynamic-update-slice_fusion.2
  171.4 0.7 fusion.49
  172.6 1.3 fusion.51
  176.2 1.0 constant_dynamic-slice_fusion.2
  178.0 0.7 copy_dynamic-update-slice_fusion.2
  178.7 0.7 fusion.49
  179.9 1.3 fusion.51
  (98 shorter events, 14.4 us)
Async XLA Ops:
  23.9 12.4 %copy-start = (s32[128]{0:T(128)S(1)}, s32[128]{0:T(128)}, u32[]{:S(2)}) copy-start(s32[128]{0:T(128)} %param.11) | copy-start | bytes 1540
  26.6 94.6 %all-to-all-start = ((bf16[2,16,256,128]{3,1,0,2:T(8,128)(2,1)}), bf16[2,16,256,128]{3,1,0,2:T(8,128)(2,1)S(1)}, u32[]{:S(2)}, u32[]{:S(2)}) async-start(bf16[2,16,256,128]{3,1,0,2:T(8,128)(2,1)} %copy.38), calls=%async_computation | async-start | bytes 4194304 | tf_op jit(solution)/shard_map/all_to_all | solution.py:64
  35.6 82.8 %all-gather.2.cloned.1.call-start = ((), (), s32[]{:S(2)}) async-start(), calls=%async_computation.1 | async-start | bytes 2359296 | tf_op jit(solution)/shard_map/all_gather | solution.py:66
Sparse Core Ops, SparseCore 0:
  39.0 79.3 all-gather.1
where the time goes:
time: 190 us; the launch traced here: 188 us
  waiting for transfers between devices  82.5 us (43%)
  local copies, waits for them, and re-layouts  27 us (14%)
  other arithmetic  22.5 us (12%)
  matrix products  18.8 us (10%)
  between operations  14.2 us (7%)
  loops' own time  13.9 us (7%)
  starting transfers between devices  9.13 us (5%)
    all_gather x1, waiting for transfers between devices, body(): gathered = lax.all_gather(steer, 'band', axis=0, tiled=True)  82 us
    dynamic_update_slice x16, other arithmetic, body(): lax.map(one_channel, jnp.arange(chan_count, dtype=jnp.int32))  15.5 us
    another operation x1, loops' own time, body(): lax.map(one_channel, jnp.arange(chan_count, dtype=jnp.int32))  13.9 us
    dot_general x1, matrix products, body(): jnp.einsum('sifk,skoc->oicf', filtered, dft_matrix_of(chan_len), preferre...  9.76 us
    all_to_all x1, starting transfers between devices, body(): lax.all_to_all(spectra, 'stn', split_axis=2, concat_axis=1, tiled=True)  8.91 us
    dynamic_slice x8, local copies, waits for them, and re-layouts, one_channel(): spectrum = lax.dynamic_index_in_dim(turned, channel, 2, keepdims=False)  7.8 us
    dot_general x8, matrix products, correlate(): lax.dot_general(stacked, stacked, (((1,), (1,)), ((), ())), preferred_ele...  5.63 us
    dynamic_slice x8, local copies, waits for them, and re-layouts, body(): lax.map(one_channel, jnp.arange(chan_count, dtype=jnp.int32))  4.42 us
  transfers between devices with their start and end apart: 2, of which 1 were waited for; matrix products, arithmetic and copies ran while one was open for 1% of the time, Pallas kernels for 0%

commit v1 on v0

v1 whole, which is shorter than its diff:
```python
import functools
import math

import jax
import jax.numpy as jnp
import numpy as np
from jax import lax
from jax.experimental import pallas as pl
from jax.experimental.pallas import tpu as pltpu
from jax.sharding import PartitionSpec as P

MESH = pl.DeviceIdType.MESH
BF16 = jnp.bfloat16
F32 = jnp.float32

STN = 32
BANDS = 8
INPUTS_HERE = 16
CHAN_HERE = 8
CHAN = 256
TAPS = 16
FRAMES = 128
SAMPLES = 36608
DIRS = 256
BEAMS = 128
STATIONS = 256
INPUTS = 512
HALF_FRAMES = 64
FIRST_COLS = (HALF_FRAMES + TAPS - 1) * CHAN
BLOCK_FRAMES = 8


def dft_rows():
    k = np.arange(CHAN)
    phase = (k[:, None] * k[None, :]) % CHAN
    angle = phase.astype(np.float32) * np.float32(2.0 * math.pi / CHAN)
    scale = np.float32(1.0 / math.sqrt(CHAN))
    c, s = np.cos(angle) * scale, np.sin(angle) * scale
    full = np.stack([np.stack([c, s], 0), np.stack([-s, c], 0)], 0)
    full = full.reshape(2, 2, CHAN, STN, CHAN_HERE).transpose(3, 0, 4, 1, 2)
    return full.reshape(2 * CHAN, 2 * CHAN).astype(jnp.bfloat16)


def pair_rows():
    return (np.arange(INPUTS)[None, :] // 2 == np.arange(STATIONS)[:, None]).astype(jnp.bfloat16)


def peer(m):
    stn = lax.axis_index("stn")
    core, z, x = stn % 2, (stn // 2) % 4, stn // 8
    far, r = (m + 1) % 2, m // 2
    dc, dz, dx = r % 2, (r // 2) % 2, r // 4
    z2 = ((z // 2 + far) % 2) * 2 + (z % 2 + dz) % 2
    to = (((x + dx) % 4) * 4 + z2) * 2 + (core + dc) % 2
    return to, (dx + far + dz + dc) == 0


def turn_kernel(
    volt_hbm, taps_ref, flags_ref, steer_hbm, dirs_ref, dft_hbm, pair_hbm,
    spec_hbm, weight_hbm,
    volt, filt, stage, parcels, table, weights, dft, pairs, keep,
    load_sem, send_sem, recv_sem, steer_send, steer_recv, local_sem,
):
    me, band = lax.axis_index("stn"), lax.axis_index("band")
    row, partner = band % 4, (band + 4) % BANDS
    column_peers = [(band // 4) * 4 + (row + d) % 4 for d in (1, 2, 3)]

    loads = []
    for s in range(2):
        for part, (start, size) in enumerate(((0, FIRST_COLS), (FIRST_COLS, SAMPLES - FIRST_COLS))):
            loads.append(pltpu.make_async_copy(
                volt_hbm.at[0, s, :, pl.ds(start, size)],
                volt.at[s, :, pl.ds(start, size)],
                load_sem.at[2 * s + part]))
    for copy in loads:
        copy.start()
    load_dft = pltpu.make_async_copy(dft_hbm, dft, load_sem.at[4])
    load_dft.start()
    load_pairs = pltpu.make_async_copy(pair_hbm, pairs, load_sem.at[5])
    load_pairs.start()

    def block(b):
        return table.at[pl.ds(pl.multiple_of(b * 512, 512), 512)]

    own_block = pltpu.make_async_copy(steer_hbm, block(band), local_sem.at[0])
    own_block.start()

    barrier = pltpu.get_barrier_semaphore()

    def greet(m, carry):
        to, here = peer(m)

        @pl.when(jnp.logical_not(here))
        def _():
            pl.semaphore_signal(barrier, inc=1, device_id=(to, band), device_id_type=MESH)

        return carry

    lax.fori_loop(0, STN, greet, 0)
    for b in column_peers + [partner]:
        pl.semaphore_signal(barrier, inc=1, device_id=(me, b), device_id_type=MESH)

    def filter_frames(s, first):
        def step(n, carry):
            f0 = first + n * BLOCK_FRAMES
            for h in range(2):
                coef = [taps_ref[t : t + 1, h * 128 : (h + 1) * 128] for t in range(TAPS)]
                acc = [None] * BLOCK_FRAMES
                for g in range(BLOCK_FRAMES + TAPS - 1):
                    at = pl.multiple_of((f0 + g) * CHAN + h * 128, 128)
                    x = volt[s, :, pl.ds(at, 128)].astype(F32)
                    for f in range(max(0, g - TAPS + 1), min(BLOCK_FRAMES - 1, g) + 1):
                        term = coef[g - f] * x
                        acc[f] = term if acc[f] is None else acc[f] + term
                for f in range(BLOCK_FRAMES):
                    to = pl.multiple_of((f0 + f) * INPUTS_HERE, INPUTS_HERE)
                    filt[s, h, pl.ds(to, INPUTS_HERE), :] = acc[f]
            return carry

        lax.fori_loop(0, HALF_FRAMES // BLOCK_FRAMES, step, 0)

    loads[0].wait()
    filter_frames(0, 0)

    pl.semaphore_wait(barrier, STN - 1 + 4)
    steer_sends = []
    for n, b in enumerate([partner] + column_peers):
        steer_sends.append(pltpu.make_async_remote_copy(
            src_ref=steer_hbm, dst_ref=block(band),
            send_sem=steer_send.at[n], recv_sem=steer_recv.at[n],
            device_id=(me, b), device_id_type=MESH))
    for copy in steer_sends:
        copy.start()

    loads[1].wait()
    filter_frames(0, HALF_FRAMES)
    loads[2].wait()
    filter_frames(1, 0)
    loads[3].wait()
    filter_frames(1, HALF_FRAMES)

    lines = lax.broadcasted_iota(jnp.int32, (INPUTS_HERE, 128), 0)
    mask = jnp.zeros((INPUTS_HERE, 128), jnp.int32)
    for i in range(INPUTS_HERE):
        mask = jnp.where(lines == i, flags_ref[i], mask)
    keep[...] = mask.astype(F32)

    load_dft.wait()

    def transform(n, carry):
        rows = []
        for i in range(2):
            parts = [filt[s, h, pl.ds(2 * n + i, FRAMES, stride=INPUTS_HERE), :]
                     for s in range(2) for h in range(2)]
            rows.append(jnp.concatenate(parts, axis=1).astype(BF16))
        out = lax.dot_general(dft[...], jnp.concatenate(rows, axis=0), (((1,), (1,)), ((), ())),
                              preferred_element_type=F32)
        for i in range(2):
            stage[pl.ds(2 * n + i, 2 * CHAN, stride=INPUTS_HERE), :] = out[:, i * 128 : (i + 1) * 128]
        return carry

    lax.fori_loop(0, INPUTS_HERE // 2, transform, 0)

    here_rows = pl.ds(pl.multiple_of(me * INPUTS_HERE, INPUTS_HERE), INPUTS_HERE)

    def parcel(m, to):
        return pltpu.make_async_remote_copy(
            src_ref=parcels.at[m], dst_ref=spec_hbm.at[:, here_rows, :],
            send_sem=send_sem.at[m], recv_sem=recv_sem.at[m],
            device_id=(to, band), device_id_type=MESH)

    def own_parcel(m):
        return pltpu.make_async_copy(parcels.at[m], spec_hbm.at[:, here_rows, :], local_sem.at[1])

    def send(m, carry):
        to, here = peer(m)
        kept = keep[...]
        for j in range(CHAN_HERE):
            for o in range(2):
                at = pl.multiple_of(to * 256 + (o * CHAN_HERE + j) * INPUTS_HERE, INPUTS_HERE)
                tile = stage[pl.ds(at, INPUTS_HERE), :] * kept
                parcels[m, j, :, o * 128 : (o + 1) * 128] = tile.astype(BF16)

        @pl.when(here)
        def _():
            own_parcel(m).start()

        @pl.when(jnp.logical_not(here))
        def _():
            parcel(m, to).start()

        return carry

    lax.fori_loop(0, STN, send, 0)

    steer_sends[0].wait_recv()
    forwards = []
    for n, b in enumerate(column_peers):
        forwards.append(pltpu.make_async_remote_copy(
            src_ref=block(partner), dst_ref=block(partner),
            send_sem=steer_send.at[4 + n], recv_sem=steer_recv.at[4 + n],
            device_id=(me, b), device_id_type=MESH))
    for copy in forwards:
        copy.start()
    own_block.wait()
    for copy in steer_sends[1:] + forwards:
        copy.wait_recv()

    def widen(n, carry):
        at = pl.multiple_of(n * 256, 256)
        rows = table[pl.ds(at, 256), :].astype(F32)
        stage[pl.ds(at, 256), :] = rows[:, :128]
        stage[pl.ds(pl.multiple_of(4096 + n * 256, 256), 256), :] = rows[:, 128:]
        return carry

    lax.fori_loop(0, 16, widen, 0)
    chosen = lax.broadcasted_iota(jnp.int32, (DIRS, BEAMS), 0) == dirs_ref[...]
    chosen = jnp.transpose(chosen.astype(F32)).astype(BF16)
    load_pairs.wait()

    def pick(n, carry):
        for o in range(2):
            halves = [stage[pl.ds(h * 4096 + o * CHAN_HERE + n, DIRS, stride=16), :] for h in range(2)]
            rows = jnp.concatenate(halves, axis=1).astype(BF16)
            picked = jnp.dot(chosen, rows, preferred_element_type=F32).astype(BF16)
            spread = jnp.dot(picked, pairs[...], preferred_element_type=F32)
            weights[n, o * BEAMS : (o + 1) * BEAMS, :] = spread.astype(BF16)
        return carry

    lax.fori_loop(0, CHAN_HERE, pick, 0)
    out_weights = pltpu.make_async_copy(weights, weight_hbm, local_sem.at[2])
    out_weights.start()

    for copy in steer_sends + forwards:
        copy.wait_send()

    def finish(m, carry):
        to, here = peer(m)

        @pl.when(here)
        def _():
            own_parcel(m).wait()

        @pl.when(jnp.logical_not(here))
        def _():
            parcel(m, to).wait()

        return carry

    lax.fori_loop(0, STN, finish, 0)
    out_weights.wait()


def form_kernel(spec_ref, weight_ref, vis_ref, beam_ref):
    rows = spec_ref[0]
    real, imag = rows[:, :FRAMES], rows[:, FRAMES:]
    turned = jnp.concatenate([imag, -real], axis=1)
    nt = (((1,), (1,)), ((), ()))
    scale = 1.0 / FRAMES
    for o, left in enumerate((rows, turned)):
        products = lax.dot_general(left, rows, nt, preferred_element_type=F32)
        vis_ref[0, 0, o] = (products * scale).astype(BF16)
    weight = weight_ref[0]
    lane = lax.broadcasted_iota(jnp.int32, weight.shape, 1)
    for p in range(2):
        mine = jnp.where(lane % 2 == p, weight, jnp.zeros_like(weight))
        formed = jnp.dot(mine, rows, preferred_element_type=F32)
        rr, ri = formed[:BEAMS, :FRAMES], formed[:BEAMS, FRAMES:]
        ir, ii = formed[BEAMS:, :FRAMES], formed[BEAMS:, FRAMES:]
        beam_ref[0, 0, 0, p] = (rr - ii).astype(BF16)
        beam_ref[0, 0, 1, p] = (ri + ir).astype(BF16)


def body(dft, pairs, voltages, taps, flags, steer, beam_dirs):
    hbm = pl.BlockSpec(memory_space=pl.ANY)
    vmem = pl.BlockSpec(memory_space=pltpu.VMEM)
    smem = pl.BlockSpec(memory_space=pltpu.SMEM)
    spectra, weights = pl.pallas_call(
        turn_kernel,
        out_shape=(
            jax.ShapeDtypeStruct((CHAN_HERE, INPUTS, 2 * FRAMES), BF16),
            jax.ShapeDtypeStruct((CHAN_HERE, 2 * BEAMS, INPUTS), BF16),
        ),
        in_specs=[hbm, vmem, smem, hbm, vmem, hbm, hbm],
        out_specs=(hbm, hbm),
        scratch_shapes=[
            pltpu.VMEM((2, INPUTS_HERE, SAMPLES), BF16),
            pltpu.VMEM((2, 2, FRAMES * INPUTS_HERE, 128), F32),
            pltpu.VMEM((2 * CHAN * INPUTS_HERE, 128), F32),
            pltpu.VMEM((STN, CHAN_HERE, INPUTS_HERE, 2 * FRAMES), BF16),
            pltpu.VMEM((DIRS * 16, STATIONS), BF16),
            pltpu.VMEM((CHAN_HERE, 2 * BEAMS, INPUTS), BF16),
            pltpu.VMEM((2 * CHAN, 2 * CHAN), BF16),
            pltpu.VMEM((STATIONS, INPUTS), BF16),
            pltpu.VMEM((INPUTS_HERE, 128), F32),
            pltpu.SemaphoreType.DMA((6,)),
            pltpu.SemaphoreType.DMA((STN,)),
            pltpu.SemaphoreType.DMA((STN,)),
            pltpu.SemaphoreType.DMA((7,)),
            pltpu.SemaphoreType.DMA((7,)),
            pltpu.SemaphoreType.DMA((3,)),
        ],
        compiler_params=pltpu.CompilerParams(
            collective_id=0, has_side_effects=True, vmem_limit_bytes=62 * 2**20
        ),
        cost_estimate=pl.CostEstimate(
            flops=1_200_000_000, bytes_accessed=12_000_000, transcendentals=0
        ),
        name="turn",
    )(voltages, taps, flags, steer.reshape(512, STATIONS), beam_dirs.reshape(1, BEAMS), dft, pairs)
    return pl.pallas_call(
        form_kernel,
        grid=(CHAN_HERE,),
        out_shape=(
            jax.ShapeDtypeStruct((1, CHAN_HERE, 2, INPUTS, INPUTS), BF16),
            jax.ShapeDtypeStruct((1, CHAN_HERE, 2, 2, BEAMS, FRAMES), BF16),
        ),
        in_specs=[
            pl.BlockSpec((1, INPUTS, 2 * FRAMES), lambda c: (c, 0, 0)),
            pl.BlockSpec((1, 2 * BEAMS, INPUTS), lambda c: (c, 0, 0)),
        ],
        out_specs=(
            pl.BlockSpec((1, 1, 2, INPUTS, INPUTS), lambda c: (0, c, 0, 0, 0)),
            pl.BlockSpec((1, 1, 2, 2, BEAMS, FRAMES), lambda c: (0, c, 0, 0, 0, 0)),
        ),
        compiler_params=pltpu.CompilerParams(vmem_limit_bytes=48 * 2**20),
        cost_estimate=pl.CostEstimate(
            flops=3_300_000_000, bytes_accessed=14_000_000, transcendentals=0
        ),
        name="form",
    )(spectra, weights)


def solution(mesh):
    dft, pairs = dft_rows(), pair_rows()

    def whole(*args):
        return jax.shard_map(
            functools.partial(body, jnp.asarray(dft), jnp.asarray(pairs)),
            mesh=mesh,
            in_specs=(P("band", None, "stn", None), P(), P("stn"), P("band", None, "stn", None), P()),
            out_specs=(P("band", "stn", None, None, None), P("band", "stn", None, None, None, None)),
            check_vma=False,
        )(*args)

    return whole
```

time: 190 us -> 80.1 us (0.42)
  waiting for transfers between devices: 82.5 us -> 0 us
  Pallas kernels: 0 us -> 76.1 us
  local copies, waits for them, and re-layouts: 27 us -> 3.17 us
  other arithmetic: 22.5 us -> 0 us
  matrix products: 18.8 us -> 0 us
  loops' own time: 13.9 us -> 0 us
  between operations: 14.2 us -> 0.65 us
  starting transfers between devices: 9.13 us -> 0 us
    all_gather x1 -> x0, waiting for transfers between devices: 82 us -> none  [body(): gathered = lax.all_gather(steer, 'band', axis=0, tiled=True)]
    pallas_call x0 -> x2, Pallas kernels: none -> 76.1 us  [the longest x1 69.6 us: body(): pl.pallas_call(turn_kernel, out_shape=(jax.ShapeDtypeStruct((CHAN_HERE, I...]
    dot_general x25 -> x0, matrix products: 18.8 us -> none  [the longest x1 9.76 us: body(): jnp.einsum('sifk,skoc->oicf', filtered, dft_matrix_of(chan_len), preferre...]
    dynamic_update_slice x16 -> x0, other arithmetic: 15.5 us -> none  [body(): lax.map(one_channel, jnp.arange(chan_count, dtype=jnp.int32))]
    another operation x1 -> x0, loops' own time: 13.9 us -> none  [body(): lax.map(one_channel, jnp.arange(chan_count, dtype=jnp.int32))]
    dynamic_slice x16 -> x0, local copies, waits for them, and re-layouts: 12.2 us -> none  [the longest x8 7.8 us: one_channel(): spectrum = lax.dynamic_index_in_dim(turned, channel, 2, keepdims=False)]
    all_to_all x1 -> x0, starting transfers between devices: 8.91 us -> none  [body(): lax.all_to_all(spectra, 'stn', split_axis=2, concat_axis=1, tiled=True)]
    another operation x11 -> x0, other arithmetic: 5.97 us -> none  [the longest x8 3.83 us: correlate(): jnp.stack([real_part, imag_part]) / frames_count]
  transfers between devices with their start and end apart: 2 -> 0, of which waited for: 1 -> 0; matrix products, arithmetic and copies ran while one was open for 1% -> 0% of each run, Pallas kernels for 0% -> 0%
where the time goes in v1:
time: 80.1 us; the launch traced here: 79.9 us
  Pallas kernels  76.1 us (95%)
  local copies, waits for them, and re-layouts  3.17 us (4%)
    pallas_call x1, Pallas kernels, body(): pl.pallas_call(turn_kernel, out_shape=(jax.ShapeDtypeStruct((CHAN_HERE, I...  69.6 us
    pallas_call x1, Pallas kernels, body(): pl.pallas_call(form_kernel, grid=(CHAN_HERE,), out_shape=(jax.ShapeDtypeS...  6.47 us
    unnamed x4, local copies, waits for them, and re-layouts  3.17 us

profile of v1, /device:TPU:35, one launch (start us, length us, event | category | flops | bytes accessed | tf_op | source)
XLA Modules:
  0.0 79.9 jit_solution(16293540922925194446)
XLA Ops:
  0.6 69.6 %turn.1 = (bf16[8,512,256]{2,1,0:T(8,128)(2,1)}, bf16[8,256,512]{2,1,0:T(8,128)(2,1)}) custom-call(bf16[1,2,16,36608]{3,2,1,0:T(8,128)(2,1)} %volt_hbm.1, f32[16,256]{1,0:T(8,128)} %taps_ref.1, s32[16]{0:T(128)} %flags_ref.1, bf16[512,256]{1,0:T(8,128)(2,1)} %bitcast.2, s32[1,128]{1,0:T(1,128)} %bitcast.3, bf16[512,512]{1,0:T(8,128)(2,1)} %constant.4.clone.dft_hbm, ...), custom_call_target="tpu_custom_call" | custom-call | flops 1200000000 | bytes 12000000 | tf_op jit(solution)/shard_map/turn/pallas_call | solution.py:278
  70.3 0.0 copy-start
  70.3 1.6 %copy-done = bf16[8,512,256]{2,1,0:T(8,128)(2,1)S(1)} copy-done((bf16[8,512,256]{2,1,0:T(8,128)(2,1)S(1)}, bf16[8,512,256]{2,1,0:T(8,128)(2,1)}, u32[]{:S(2)}) %copy-start) | copy-done | bytes 2097176
  71.9 0.0 copy-start.1
  71.9 1.6 %copy-done.1 = bf16[8,256,512]{2,1,0:T(8,128)(2,1)S(1)} copy-done((bf16[8,256,512]{2,1,0:T(8,128)(2,1)S(1)}, bf16[8,256,512]{2,1,0:T(8,128)(2,1)}, u32[]{:S(2)}) %copy-start.1) | copy-done | bytes 2097176
  73.4 6.5 %form.1 = (bf16[1,8,2,512,512]{4,3,2,1,0:T(8,128)(2,1)}, bf16[1,8,2,2,128,128]{5,4,3,2,1,0:T(8,128)(2,1)}) custom-call(bf16[8,512,256]{2,1,0:T(8,128)(2,1)S(1)} %copy-done, bf16[8,256,512]{2,1,0:T(8,128)(2,1)S(1)} %copy-done.1), custom_call_target="tpu_custom_call" | custom-call | flops 3300000000 | bytes 14000000 | tf_op jit(solution)/shard_map/form/pallas_call | solution.py:311
Async XLA Ops:
  70.3 1.6 %copy-start = (bf16[8,512,256]{2,1,0:T(8,128)(2,1)S(1)}, bf16[8,512,256]{2,1,0:T(8,128)(2,1)}, u32[]{:S(2)}) copy-start(bf16[8,512,256]{2,1,0:T(8,128)(2,1)} %get-tuple-element.4.spec_ref) | copy-start | bytes 6291460
  71.9 1.6 %copy-start.1 = (bf16[8,256,512]{2,1,0:T(8,128)(2,1)S(1)}, bf16[8,256,512]{2,1,0:T(8,128)(2,1)}, u32[]{:S(2)}) copy-start(bf16[8,256,512]{2,1,0:T(8,128)(2,1)} %get-tuple-element.5.weight_ref) | copy-start | bytes 6291460

commit v2 on v1

--- a/solution.py
+++ b/solution.py
@@ -41,10 +41,6 @@
     return full.reshape(2 * CHAN, 2 * CHAN).astype(jnp.bfloat16)
 
 
-def pair_rows():
-    return (np.arange(INPUTS)[None, :] // 2 == np.arange(STATIONS)[:, None]).astype(jnp.bfloat16)
-
-
 def peer(m):
     stn = lax.axis_index("stn")
     core, z, x = stn % 2, (stn // 2) % 4, stn // 8
@@ -56,9 +52,9 @@
 
 
 def turn_kernel(
-    volt_hbm, taps_ref, flags_ref, steer_hbm, dirs_ref, dft_hbm, pair_hbm,
+    volt_hbm, taps_ref, flags_ref, steer_hbm, dirs_ref, dft_hbm,
     spec_hbm, weight_hbm,
-    volt, filt, stage, parcels, table, weights, dft, pairs, keep,
+    volt, filt, stage, parcels, table, weights, dft, keep,
     load_sem, send_sem, recv_sem, steer_send, steer_recv, local_sem,
 ):
     me, band = lax.axis_index("stn"), lax.axis_index("band")
@@ -76,8 +72,6 @@
         copy.start()
     load_dft = pltpu.make_async_copy(dft_hbm, dft, load_sem.at[4])
     load_dft.start()
-    load_pairs = pltpu.make_async_copy(pair_hbm, pairs, load_sem.at[5])
-    load_pairs.start()
 
     def block(b):
         return table.at[pl.ds(pl.multiple_of(b * 512, 512), 512)]
@@ -216,14 +210,15 @@
     lax.fori_loop(0, 16, widen, 0)
     chosen = lax.broadcasted_iota(jnp.int32, (DIRS, BEAMS), 0) == dirs_ref[...]
     chosen = jnp.transpose(chosen.astype(F32)).astype(BF16)
-    load_pairs.wait()
+    pairs = (lax.broadcasted_iota(jnp.int32, (STATIONS, INPUTS), 1) // 2
+             == lax.broadcasted_iota(jnp.int32, (STATIONS, INPUTS), 0)).astype(F32).astype(BF16)
 
     def pick(n, carry):
         for o in range(2):
             halves = [stage[pl.ds(h * 4096 + o * CHAN_HERE + n, DIRS, stride=16), :] for h in range(2)]
             rows = jnp.concatenate(halves, axis=1).astype(BF16)
             picked = jnp.dot(chosen, rows, preferred_element_type=F32).astype(BF16)
-            spread = jnp.dot(picked, pairs[...], preferred_element_type=F32)
+            spread = jnp.dot(picked, pairs, preferred_element_type=F32)
             weights[n, o * BEAMS : (o + 1) * BEAMS, :] = spread.astype(BF16)
         return carry
 
@@ -251,28 +246,37 @@
     out_weights.wait()
 
 
-def form_kernel(spec_ref, weight_ref, vis_ref, beam_ref):
-    rows = spec_ref[0]
-    real, imag = rows[:, :FRAMES], rows[:, FRAMES:]
-    turned = jnp.concatenate([imag, -real], axis=1)
+def form_kernel(spec_ref, weight_ref, vis_hbm, beam_hbm, vis, beam, vis_sem, beam_sem):
     nt = (((1,), (1,)), ((), ()))
     scale = 1.0 / FRAMES
-    for o, left in enumerate((rows, turned)):
-        products = lax.dot_general(left, rows, nt, preferred_element_type=F32)
-        vis_ref[0, 0, o] = (products * scale).astype(BF16)
-    weight = weight_ref[0]
-    lane = lax.broadcasted_iota(jnp.int32, weight.shape, 1)
-    for p in range(2):
-        mine = jnp.where(lane % 2 == p, weight, jnp.zeros_like(weight))
-        formed = jnp.dot(mine, rows, preferred_element_type=F32)
-        rr, ri = formed[:BEAMS, :FRAMES], formed[:BEAMS, FRAMES:]
-        ir, ii = formed[BEAMS:, :FRAMES], formed[BEAMS:, FRAMES:]
-        beam_ref[0, 0, 0, p] = (rr - ii).astype(BF16)
-        beam_ref[0, 0, 1, p] = (ri + ir).astype(BF16)
-
-
-def body(dft, pairs, voltages, taps, flags, steer, beam_dirs):
-    hbm = pl.BlockSpec(memory_space=pl.ANY)
+    lane = lax.broadcasted_iota(jnp.int32, (2 * BEAMS, INPUTS), 1)
+    writes = []
+    for c in range(CHAN_HERE):
+        rows = spec_ref[c]
+        real, imag = rows[:, :FRAMES], rows[:, FRAMES:]
+        for o in range(2):
+            left = rows if o == 0 else jnp.concatenate([imag, -real], axis=1)
+            products = lax.dot_general(left, rows, nt, preferred_element_type=F32)
+            vis[c, o] = (products * scale).astype(BF16)
+            writes.append(pltpu.make_async_copy(vis.at[c, o], vis_hbm.at[0, c, o], vis_sem.at[c, o]))
+            writes[-1].start()
+        weight = weight_ref[c]
+        for p in range(2):
+            mine = jnp.where(lane % 2 == p, weight, jnp.zeros_like(weight))
+            formed = jnp.dot(mine, rows, preferred_element_type=F32)
+            rr, ri = formed[:BEAMS, :FRAMES], formed[:BEAMS, FRAMES:]
+            ir, ii = formed[BEAMS:, :FRAMES], formed[BEAMS:, FRAMES:]
+            beam[c, 0, p] = (rr - ii).astype(BF16)
+            beam[c, 1, p] = (ri + ir).astype(BF16)
+        writes.append(pltpu.make_async_copy(beam.at[c], beam_hbm.at[0, c], beam_sem.at[c]))
+        writes[-1].start()
+    for copy in writes:
+        copy.wait()
+
+
+def body(dft, voltages, taps, flags, steer, beam_dirs):
+    hbm = pl.BlockSpec(memory_space=pltpu.HBM)
+    anywhere = pl.BlockSpec(memory_space=pl.ANY)
     vmem = pl.BlockSpec(memory_space=pltpu.VMEM)
     smem = pl.BlockSpec(memory_space=pltpu.SMEM)
     spectra, weights = pl.pallas_call(
@@ -281,8 +285,8 @@
             jax.ShapeDtypeStruct((CHAN_HERE, INPUTS, 2 * FRAMES), BF16),
             jax.ShapeDtypeStruct((CHAN_HERE, 2 * BEAMS, INPUTS), BF16),
         ),
-        in_specs=[hbm, vmem, smem, hbm, vmem, hbm, hbm],
-        out_specs=(hbm, hbm),
+        in_specs=[hbm, vmem, smem, hbm, vmem, anywhere],
+        out_specs=(anywhere, anywhere),
         scratch_shapes=[
             pltpu.VMEM((2, INPUTS_HERE, SAMPLES), BF16),
             pltpu.VMEM((2, 2, FRAMES * INPUTS_HERE, 128), F32),
@@ -291,9 +295,8 @@
             pltpu.VMEM((DIRS * 16, STATIONS), BF16),
             pltpu.VMEM((CHAN_HERE, 2 * BEAMS, INPUTS), BF16),
             pltpu.VMEM((2 * CHAN, 2 * CHAN), BF16),
-            pltpu.VMEM((STATIONS, INPUTS), BF16),
             pltpu.VMEM((INPUTS_HERE, 128), F32),
-            pltpu.SemaphoreType.DMA((6,)),
+            pltpu.SemaphoreType.DMA((5,)),
             pltpu.SemaphoreType.DMA((STN,)),
             pltpu.SemaphoreType.DMA((STN,)),
             pltpu.SemaphoreType.DMA((7,)),
@@ -301,29 +304,29 @@
             pltpu.SemaphoreType.DMA((3,)),
         ],
         compiler_params=pltpu.CompilerParams(
-            collective_id=0, has_side_effects=True, vmem_limit_bytes=62 * 2**20
+            collective_id=0, has_side_effects=True, vmem_limit_bytes=36 * 2**20
         ),
         cost_estimate=pl.CostEstimate(
             flops=1_200_000_000, bytes_accessed=12_000_000, transcendentals=0
         ),
         name="turn",
-    )(voltages, taps, flags, steer.reshape(512, STATIONS), beam_dirs.reshape(1, BEAMS), dft, pairs)
+    )(*[pltpu.with_memory_space_constraint(v, pltpu.HBM) for v in (
+        voltages, taps, flags, steer.reshape(512, STATIONS), beam_dirs.reshape(1, BEAMS), dft)])
     return pl.pallas_call(
         form_kernel,
-        grid=(CHAN_HERE,),
         out_shape=(
             jax.ShapeDtypeStruct((1, CHAN_HERE, 2, INPUTS, INPUTS), BF16),
             jax.ShapeDtypeStruct((1, CHAN_HERE, 2, 2, BEAMS, FRAMES), BF16),
         ),
-        in_specs=[
-            pl.BlockSpec((1, INPUTS, 2 * FRAMES), lambda c: (c, 0, 0)),
-            pl.BlockSpec((1, 2 * BEAMS, INPUTS), lambda c: (c, 0, 0)),
+        in_specs=[vmem, vmem],
+        out_specs=(anywhere, anywhere),
+        scratch_shapes=[
+            pltpu.VMEM((CHAN_HERE, 2, INPUTS, INPUTS), BF16),
+            pltpu.VMEM((CHAN_HERE, 2, 2, BEAMS, FRAMES), BF16),
+            pltpu.SemaphoreType.DMA((CHAN_HERE, 2)),
+            pltpu.SemaphoreType.DMA((CHAN_HERE,)),
         ],
-        out_specs=(
-            pl.BlockSpec((1, 1, 2, INPUTS, INPUTS), lambda c: (0, c, 0, 0, 0)),
-            pl.BlockSpec((1, 1, 2, 2, BEAMS, FRAMES), lambda c: (0, c, 0, 0, 0, 0)),
-        ),
-        compiler_params=pltpu.CompilerParams(vmem_limit_bytes=48 * 2**20),
+        compiler_params=pltpu.CompilerParams(vmem_limit_bytes=32 * 2**20),
         cost_estimate=pl.CostEstimate(
             flops=3_300_000_000, bytes_accessed=14_000_000, transcendentals=0
         ),
@@ -332,11 +335,11 @@
 
 
 def solution(mesh):
-    dft, pairs = dft_rows(), pair_rows()
+    dft = dft_rows()
 
     def whole(*args):
         return jax.shard_map(
-            functools.partial(body, jnp.asarray(dft), jnp.asarray(pairs)),
+            functools.partial(body, jnp.asarray(dft)),
             mesh=mesh,
             in_specs=(P("band", None, "stn", None), P(), P("stn"), P("band", None, "stn", None), P()),
             out_specs=(P("band", "stn", None, None, None), P("band", "stn", None, None, None, None)),

time: 80.1 us -> 74.7 us (0.933)
  local copies, waits for them, and re-layouts: 3.17 us -> 0 us
  Pallas kernels: 76.1 us -> 73.9 us
    unnamed x4 -> x0, local copies, waits for them, and re-layouts: 3.17 us -> none
    pallas_call x1, Pallas kernels: 6.47 us -> 4.39 us  [body(): pl.pallas_call(form_kernel, out_shape=(jax.ShapeDtypeStruct((1, CHAN_HERE...]
where the time goes in v2:
time: 74.7 us; the launch traced here: 74.5 us
  Pallas kernels  73.9 us (99%)
    pallas_call x1, Pallas kernels, body(): pl.pallas_call(turn_kernel, out_shape=(jax.ShapeDtypeStruct((CHAN_HERE, I...  69.5 us
    pallas_call x1, Pallas kernels, body(): pl.pallas_call(form_kernel, out_shape=(jax.ShapeDtypeStruct((1, CHAN_HERE...  4.39 us

profile of v2, /device:TPU:35, one launch (start us, length us, event | category | flops | bytes accessed | tf_op | source)
XLA Modules:
  0.0 74.5 jit_solution(5945583655525895018)
XLA Ops:
  0.6 69.5 %turn.1 = (bf16[8,512,256]{2,1,0:T(8,128)(2,1)S(1)}, bf16[8,256,512]{2,1,0:T(8,128)(2,1)S(1)}) custom-call(bf16[1,2,16,36608]{3,2,1,0:T(8,128)(2,1)} %volt_hbm.1, f32[16,256]{1,0:T(8,128)} %taps_ref.1, s32[16]{0:T(128)} %flags_ref.1, bf16[512,256]{1,0:T(8,128)(2,1)} %bitcast.2, s32[1,128]{1,0:T(1,128)} %bitcast.3, bf16[512,512]{1,0:T(8,128)(2,1)} %constant.2.clone.dft_hbm), custom_call_target="tpu_custom_call" | custom-call | flops 1200000000 | bytes 12000000 | tf_op jit(solution)/shard_map/turn/pallas_call | solution.py:282
  70.1 4.4 %form.1 = (bf16[1,8,2,512,512]{4,3,2,1,0:T(8,128)(2,1)}, bf16[1,8,2,2,128,128]{5,4,3,2,1,0:T(8,128)(2,1)}) custom-call(bf16[8,512,256]{2,1,0:T(8,128)(2,1)S(1)} %get-tuple-element.4.spec_ref, bf16[8,256,512]{2,1,0:T(8,128)(2,1)S(1)} %get-tuple-element.5.weight_ref), custom_call_target="tpu_custom_call" | custom-call | flops 3300000000 | bytes 14000000 | tf_op jit(solution)/shard_map/form/pallas_call | solution.py:315

commit v3 on v2

--- a/solution.py
+++ b/solution.py
@@ -27,7 +27,7 @@
 INPUTS = 512
 HALF_FRAMES = 64
 FIRST_COLS = (HALF_FRAMES + TAPS - 1) * CHAN
-BLOCK_FRAMES = 8
+BLOCK_FRAMES = 16
 
 
 def dft_rows():
@@ -52,15 +52,33 @@
 
 
 def turn_kernel(
-    volt_hbm, taps_ref, flags_ref, steer_hbm, dirs_ref, dft_hbm,
+    volt_hbm, taps_hbm, flags_hbm, steer_hbm, dirs_hbm, dft_hbm,
     spec_hbm, weight_hbm,
-    volt, filt, stage, parcels, table, weights, dft, keep,
+    volt, filt, stage, parcels, table, weights, dft, keep, taps_ref, flags_ref, dirs_ref,
     load_sem, send_sem, recv_sem, steer_send, steer_recv, local_sem,
 ):
     me, band = lax.axis_index("stn"), lax.axis_index("band")
     row, partner = band % 4, (band + 4) % BANDS
     column_peers = [(band // 4) * 4 + (row + d) % 4 for d in (1, 2, 3)]
 
+    barrier = pltpu.get_barrier_semaphore()
+    for b in [partner] + column_peers:
+        pl.semaphore_signal(barrier, inc=1, device_id=(me, b), device_id_type=MESH)
+
+    def greet(to, carry):
+        @pl.when(to != me)
+        def _():
+            pl.semaphore_signal(barrier, inc=1, device_id=(to, band), device_id_type=MESH)
+
+        return carry
+
+    lax.fori_loop(0, STN, greet, 0)
+
+    load_taps = pltpu.make_async_copy(taps_hbm, taps_ref, load_sem.at[5])
+    load_flags = pltpu.make_async_copy(flags_hbm, flags_ref, load_sem.at[6])
+    load_dirs = pltpu.make_async_copy(dirs_hbm, dirs_ref, load_sem.at[7])
+    for copy in (load_taps, load_flags, load_dirs):
+        copy.start()
     loads = []
     for s in range(2):
         for part, (start, size) in enumerate(((0, FIRST_COLS), (FIRST_COLS, SAMPLES - FIRST_COLS))):
@@ -78,21 +96,6 @@
 
     own_block = pltpu.make_async_copy(steer_hbm, block(band), local_sem.at[0])
     own_block.start()
-
-    barrier = pltpu.get_barrier_semaphore()
-
-    def greet(m, carry):
-        to, here = peer(m)
-
-        @pl.when(jnp.logical_not(here))
-        def _():
-            pl.semaphore_signal(barrier, inc=1, device_id=(to, band), device_id_type=MESH)
-
-        return carry
-
-    lax.fori_loop(0, STN, greet, 0)
-    for b in column_peers + [partner]:
-        pl.semaphore_signal(barrier, inc=1, device_id=(me, b), device_id_type=MESH)
 
     def filter_frames(s, first):
         def step(n, carry):
@@ -113,9 +116,6 @@
 
         lax.fori_loop(0, HALF_FRAMES // BLOCK_FRAMES, step, 0)
 
-    loads[0].wait()
-    filter_frames(0, 0)
-
     pl.semaphore_wait(barrier, STN - 1 + 4)
     steer_sends = []
     for n, b in enumerate([partner] + column_peers):
@@ -126,6 +126,9 @@
     for copy in steer_sends:
         copy.start()
 
+    load_taps.wait()
+    loads[0].wait()
+    filter_frames(0, 0)
     loads[1].wait()
     filter_frames(0, HALF_FRAMES)
     loads[2].wait()
@@ -133,6 +136,7 @@
     loads[3].wait()
     filter_frames(1, HALF_FRAMES)
 
+    load_flags.wait()
     lines = lax.broadcasted_iota(jnp.int32, (INPUTS_HERE, 128), 0)
     mask = jnp.zeros((INPUTS_HERE, 128), jnp.int32)
     for i in range(INPUTS_HERE):
@@ -141,19 +145,14 @@
 
     load_dft.wait()
 
-    def transform(n, carry):
-        rows = []
-        for i in range(2):
-            parts = [filt[s, h, pl.ds(2 * n + i, FRAMES, stride=INPUTS_HERE), :]
-                     for s in range(2) for h in range(2)]
-            rows.append(jnp.concatenate(parts, axis=1).astype(BF16))
-        out = lax.dot_general(dft[...], jnp.concatenate(rows, axis=0), (((1,), (1,)), ((), ())),
-                              preferred_element_type=F32)
-        for i in range(2):
-            stage[pl.ds(2 * n + i, 2 * CHAN, stride=INPUTS_HERE), :] = out[:, i * 128 : (i + 1) * 128]
-        return carry
-
-    lax.fori_loop(0, INPUTS_HERE // 2, transform, 0)
+    rows = []
+    for i in range(INPUTS_HERE):
+        parts = [filt[s, h, pl.ds(i, FRAMES, stride=INPUTS_HERE), :] for s in range(2) for h in range(2)]
+        rows.append(jnp.concatenate(parts, axis=1).astype(BF16))
+    out = lax.dot_general(dft[...], jnp.concatenate(rows, axis=0), (((1,), (1,)), ((), ())),
+                          preferred_element_type=F32)
+    for i in range(INPUTS_HERE):
+        stage[pl.ds(i, 2 * CHAN, stride=INPUTS_HERE), :] = out[:, i * 128 : (i + 1) * 128]
 
     here_rows = pl.ds(pl.multiple_of(me * INPUTS_HERE, INPUTS_HERE), INPUTS_HERE)
 
@@ -208,6 +207,7 @@
         return carry
 
     lax.fori_loop(0, 16, widen, 0)
+    load_dirs.wait()
     chosen = lax.broadcasted_iota(jnp.int32, (DIRS, BEAMS), 0) == dirs_ref[...]
     chosen = jnp.transpose(chosen.astype(F32)).astype(BF16)
     pairs = (lax.broadcasted_iota(jnp.int32, (STATIONS, INPUTS), 1) // 2
@@ -278,14 +278,13 @@
     hbm = pl.BlockSpec(memory_space=pltpu.HBM)
     anywhere = pl.BlockSpec(memory_space=pl.ANY)
     vmem = pl.BlockSpec(memory_space=pltpu.VMEM)
-    smem = pl.BlockSpec(memory_space=pltpu.SMEM)
     spectra, weights = pl.pallas_call(
         turn_kernel,
         out_shape=(
             jax.ShapeDtypeStruct((CHAN_HERE, INPUTS, 2 * FRAMES), BF16),
             jax.ShapeDtypeStruct((CHAN_HERE, 2 * BEAMS, INPUTS), BF16),
         ),
-        in_specs=[hbm, vmem, smem, hbm, vmem, anywhere],
+        in_specs=[hbm] * 6,
         out_specs=(anywhere, anywhere),
         scratch_shapes=[
             pltpu.VMEM((2, INPUTS_HERE, SAMPLES), BF16),
@@ -296,7 +295,10 @@
             pltpu.VMEM((CHAN_HERE, 2 * BEAMS, INPUTS), BF16),
             pltpu.VMEM((2 * CHAN, 2 * CHAN), BF16),
             pltpu.VMEM((INPUTS_HERE, 128), F32),
-            pltpu.SemaphoreType.DMA((5,)),
+            pltpu.VMEM((TAPS, CHAN), F32),
+            pltpu.SMEM((INPUTS_HERE,), jnp.int32),
+            pltpu.VMEM((1, BEAMS), jnp.int32),
+            pltpu.SemaphoreType.DMA((8,)),
             pltpu.SemaphoreType.DMA((STN,)),
             pltpu.SemaphoreType.DMA((STN,)),
             pltpu.SemaphoreType.DMA((7,)),

time: 74.7 us -> 71.9 us (0.963)
  Pallas kernels: 73.9 us -> 71.2 us
    pallas_call x1, Pallas kernels: 69.5 us -> 66.8 us  [body(): pl.pallas_call(turn_kernel, out_shape=(jax.ShapeDtypeStruct((CHAN_HERE, I...]
where the time goes in v3:
time: 71.9 us; the launch traced here: 71.8 us
  Pallas kernels  71.2 us (99%)
    pallas_call x1, Pallas kernels, body(): pl.pallas_call(turn_kernel, out_shape=(jax.ShapeDtypeStruct((CHAN_HERE, I...  66.8 us
    pallas_call x1, Pallas kernels, body(): pl.pallas_call(form_kernel, out_shape=(jax.ShapeDtypeStruct((1, CHAN_HERE...  4.39 us

profile of v3, /device:TPU:35, one launch (start us, length us, event | category | flops | bytes accessed | tf_op | source)
XLA Modules:
  0.0 71.8 jit_solution(2734072403814236860)
XLA Ops:
  0.6 66.8 %turn.1 = (bf16[8,512,256]{2,1,0:T(8,128)(2,1)S(1)}, bf16[8,256,512]{2,1,0:T(8,128)(2,1)S(1)}) custom-call(bf16[1,2,16,36608]{3,2,1,0:T(8,128)(2,1)} %volt_hbm.1, f32[16,256]{1,0:T(8,128)} %taps_hbm.1, s32[16]{0:T(128)} %flags_hbm.1, bf16[512,256]{1,0:T(8,128)(2,1)} %bitcast.2, s32[1,128]{1,0:T(1,128)} %bitcast.3, bf16[512,512]{1,0:T(8,128)(2,1)} %constant.2.clone.dft_hbm), custom_call_target="tpu_custom_call" | custom-call | flops 1200000000 | bytes 12000000 | tf_op jit(solution)/shard_map/turn/pallas_call | solution.py:281
  67.4 4.4 %form.1 = (bf16[1,8,2,512,512]{4,3,2,1,0:T(8,128)(2,1)}, bf16[1,8,2,2,128,128]{5,4,3,2,1,0:T(8,128)(2,1)}) custom-call(bf16[8,512,256]{2,1,0:T(8,128)(2,1)S(1)} %get-tuple-element.4.spec_ref, bf16[8,256,512]{2,1,0:T(8,128)(2,1)S(1)} %get-tuple-element.5.weight_ref), custom_call_target="tpu_custom_call" | custom-call | flops 3300000000 | bytes 14000000 | tf_op jit(solution)/shard_map/form/pallas_call | solution.py:317

commit v4 on v3

--- a/solution.py
+++ b/solution.py
@@ -45,7 +45,7 @@
     stn = lax.axis_index("stn")
     core, z, x = stn % 2, (stn // 2) % 4, stn // 8
     far, r = (m + 1) % 2, m // 2
-    dc, dz, dx = r % 2, (r // 2) % 2, r // 4
+    dc, dz, dx = r % 2, (r // 2) % 2, 3 - r // 4
     z2 = ((z // 2 + far) % 2) * 2 + (z % 2 + dz) % 2
     to = (((x + dx) % 4) * 4 + z2) * 2 + (core + dc) % 2
     return to, (dx + far + dz + dc) == 0
@@ -65,14 +65,8 @@
     for b in [partner] + column_peers:
         pl.semaphore_signal(barrier, inc=1, device_id=(me, b), device_id_type=MESH)
 
-    def greet(to, carry):
-        @pl.when(to != me)
-        def _():
-            pl.semaphore_signal(barrier, inc=1, device_id=(to, band), device_id_type=MESH)
-
-        return carry
-
-    lax.fori_loop(0, STN, greet, 0)
+    for n in range(1, STN):
+        pl.semaphore_signal(barrier, inc=1, device_id=((me + n) % STN, band), device_id_type=MESH)
 
     load_taps = pltpu.make_async_copy(taps_hbm, taps_ref, load_sem.at[5])
     load_flags = pltpu.make_async_copy(flags_hbm, flags_ref, load_sem.at[6])

time: 71.9 us -> 71.4 us (level)
  Pallas kernels: 71.2 us -> 70.2 us
    pallas_call x1, Pallas kernels: 66.8 us -> 65.8 us  [body(): pl.pallas_call(turn_kernel, out_shape=(jax.ShapeDtypeStruct((CHAN_HERE, I...]
where the time goes in v4:
time: 71.4 us; the launch traced here: 70.8 us
  Pallas kernels  70.2 us (98%)
    pallas_call x1, Pallas kernels, body(): pl.pallas_call(turn_kernel, out_shape=(jax.ShapeDtypeStruct((CHAN_HERE, I...  65.8 us
    pallas_call x1, Pallas kernels, body(): pl.pallas_call(form_kernel, out_shape=(jax.ShapeDtypeStruct((1, CHAN_HERE...  4.39 us

profile of v4, /device:TPU:35, one launch (start us, length us, event | category | flops | bytes accessed | tf_op | source)
XLA Modules:
  0.0 70.8 jit_solution(14632996342768455526)
XLA Ops:
  0.6 65.8 %turn.1 = (bf16[8,512,256]{2,1,0:T(8,128)(2,1)S(1)}, bf16[8,256,512]{2,1,0:T(8,128)(2,1)S(1)}) custom-call(bf16[1,2,16,36608]{3,2,1,0:T(8,128)(2,1)} %volt_hbm.1, f32[16,256]{1,0:T(8,128)} %taps_hbm.1, s32[16]{0:T(128)} %flags_hbm.1, bf16[512,256]{1,0:T(8,128)(2,1)} %bitcast.2, s32[1,128]{1,0:T(1,128)} %bitcast.3, bf16[512,512]{1,0:T(8,128)(2,1)} %constant.2.clone.dft_hbm), custom_call_target="tpu_custom_call" | custom-call | flops 1200000000 | bytes 12000000 | tf_op jit(solution)/shard_map/turn/pallas_call | solution.py:275
  66.4 4.4 %form.1 = (bf16[1,8,2,512,512]{4,3,2,1,0:T(8,128)(2,1)}, bf16[1,8,2,2,128,128]{5,4,3,2,1,0:T(8,128)(2,1)}) custom-call(bf16[8,512,256]{2,1,0:T(8,128)(2,1)S(1)} %get-tuple-element.4.spec_ref, bf16[8,256,512]{2,1,0:T(8,128)(2,1)S(1)} %get-tuple-element.5.weight_ref), custom_call_target="tpu_custom_call" | custom-call | flops 3300000000 | bytes 14000000 | tf_op jit(solution)/shard_map/form/pallas_call | solution.py:311
